TPU v7x, 32 devices: a whole 2x2x4 slice. The times are simulated.
32 devices in a mesh: dp: 8 (over y, x, core), tensor: 4 (over z).
Axes of the slice: x: 2, y: 2, z: 4, core: 2. Of those that a mesh axis runs over, the one named last changes fastest.
Arguments:
- patches: bfloat16 [16384, 1024], P('dp'), may hold values from -6 to 6
- pos_embed: bfloat16 [16384, 1024], P('dp'), may hold values from -6 to 6
- counts: int32 [8, 8], P('dp'), may hold values from 96 to 576, as said below
- ln1_gain: float32 [1024], replicated, may hold values from 0.5 to 1.5
- w_qkv: bfloat16 [1024, 3, 1024], P(None, None, 'tensor'), may hold values from -0.1875 to 0.1875
- w_out: bfloat16 [1024, 1024], P('tensor'), may hold values from -0.75 to 0.75
- ln2_gain: float32 [1024], replicated, may hold values from 0.5 to 1.5
- w_up: bfloat16 [1024, 4096], P(None, 'tensor'), may hold values from -0.1875 to 0.1875
- w_down: bfloat16 [4096, 1024], P('tensor'), may hold values from -0.09375 to 0.09375
- ln3_gain: float32 [1024], replicated, may hold values from 0.5 to 1.5
- w_learn1: bfloat16 [1024, 1024], replicated, may hold values from -0.1875 to 0.1875
- w_learn2: bfloat16 [1024, 8], replicated, may hold values from -0.1875 to 0.1875
- cotangent: bfloat16 [64, 8, 1024], P('dp'), may hold values from -48 to 48
Outputs:
- learned: bfloat16 [64, 8, 1024], P('dp')
- input_grad: bfloat16 [16384, 1024], P('dp')
- grad_ln1_gain: float32 [1024], replicated
- grad_w_qkv: float32 [1024, 3, 1024], P(None, None, 'tensor')
- grad_w_out: float32 [1024, 1024], P('tensor')
- grad_ln2_gain: float32 [1024], replicated
- grad_w_up: float32 [1024, 4096], P(None, 'tensor')
- grad_w_down: float32 [4096, 1024], P('tensor')
- grad_ln3_gain: float32 [1024], replicated
- grad_w_learn1: float32 [1024, 1024], replicated
- grad_w_learn2: float32 [1024, 8], replicated
Inputs may be any that keep to these rules, and one draw needn't show every extreme that they name: Each row of 8 counts sums to 2048, and the largest of each row is 576.
All inputs are finite; a program needn't handle non-finite values.
Results may differ from a plain program's by a relative error of at most 0.019.
Values may be sent and summed in bfloat16 or wider, within the bound.
No kernel may reach another device: no remote copies, remote signals or barrier semaphores. Data moves between devices by JAX's collectives and lax.ppermute only.
A program may use at most 256 MiB of HBM per device.

v0:
```python
import jax
import jax.numpy as jnp
from jax import lax
from jax.sharding import PartitionSpec as P

HEAD_DIM = 64
MOST = 576
BLOCK = 512
WINDOW = 1664
EPSILON = 1e-06
LOW_TYPE = jnp.bfloat16
WIDE_TYPE = jnp.float32


def layer_norm(values, gain_vector):
    center = values - jnp.mean(values, axis=-1, keepdims=True)
    variance = jnp.mean(center * center, axis=-1, keepdims=True)
    inverse = lax.rsqrt(variance + EPSILON)
    normed = center * inverse
    return (normed * gain_vector, normed, inverse)


def norm_back(grad_in, gain_vector, normed, inverse):
    gain_grad = jnp.sum(grad_in * normed, axis=0)
    scaled = grad_in * gain_vector
    result = (
        scaled
        - jnp.mean(scaled, axis=-1, keepdims=True)
        - normed * jnp.mean(scaled * normed, axis=-1, keepdims=True)
    ) * inverse
    return (result, gain_grad)


def gelu_exact(values):
    return jax.nn.gelu(values, approximate=False)


def gelu_grad(values, upstream):
    pullback = jax.vjp(gelu_exact, values)[1]
    return pullback(upstream)[0]


def image_ids(counts_row, row_count):
    ends = jnp.cumsum(counts_row)
    places = jnp.arange(row_count, dtype=jnp.int32)
    return jnp.sum((places[:, None] >= ends[None, :]).astype(jnp.int32), axis=1)


def block_pieces(query, keys, values, image_of, block_index, score_scale):
    row_count = query.shape[0]
    query_start = block_index * BLOCK
    key_start = jnp.clip(query_start - MOST, 0, row_count - WINDOW)
    query_block = lax.dynamic_slice_in_dim(query, query_start, BLOCK, 0)
    key_block = lax.dynamic_slice_in_dim(keys, key_start, WINDOW, 0)
    value_block = lax.dynamic_slice_in_dim(values, key_start, WINDOW, 0)
    query_ids = lax.dynamic_slice_in_dim(image_of, query_start, BLOCK, 0)
    key_ids = lax.dynamic_slice_in_dim(image_of, key_start, WINDOW, 0)
    scores = (
        jnp.einsum("qhd,khd->hqk", query_block, key_block, preferred_element_type=WIDE_TYPE)
        * score_scale
    )
    allowed = (query_ids[:, None] == key_ids[None, :])[None]
    scores = jnp.where(allowed, scores, -1e30)
    return (query_start, key_start, query_block, key_block, value_block, scores)


def attend_forward(query, keys, values, image_of, score_scale):
    row_count = query.shape[0]

    def one_block(block_index):
        pieces = block_pieces(query, keys, values, image_of, block_index, score_scale)
        value_block = pieces[4]
        scores = pieces[5]
        row_max = jnp.max(scores, axis=-1, keepdims=True)
        exponent = jnp.exp(scores - row_max)
        row_total = jnp.sum(exponent, axis=-1, keepdims=True)
        probs = (exponent / row_total).astype(LOW_TYPE)
        result = jnp.einsum("hqk,khd->qhd", probs, value_block, preferred_element_type=WIDE_TYPE)
        return (result.astype(LOW_TYPE), row_max + jnp.log(row_total))

    outputs, log_sums = lax.map(one_block, jnp.arange(row_count // BLOCK, dtype=jnp.int32))
    return (outputs.reshape(query.shape), log_sums)


def attend_backward(query, keys, values, image_of, log_sums, grad_mixed, score_scale):
    row_count = query.shape[0]

    def one_block(block_index, carried):
        grad_query, grad_keys, grad_values = carried
        pieces = block_pieces(query, keys, values, image_of, block_index, score_scale)
        query_start, key_start, query_block, key_block, value_block, scores = pieces
        grad_block = lax.dynamic_slice_in_dim(grad_mixed, query_start, BLOCK, 0)
        probs = jnp.exp(scores - log_sums[block_index])
        grad_probs = jnp.einsum(
            "qhd,khd->hqk", grad_block, value_block, preferred_element_type=WIDE_TYPE
        )
        inner_sum = jnp.sum(probs * grad_probs, axis=-1, keepdims=True)
        grad_scores = (probs * (grad_probs - inner_sum)).astype(LOW_TYPE)
        query_part = (
            jnp.einsum("hqk,khd->qhd", grad_scores, key_block, preferred_element_type=WIDE_TYPE)
            * score_scale
        )
        key_part = (
            jnp.einsum("hqk,qhd->khd", grad_scores, query_block, preferred_element_type=WIDE_TYPE)
            * score_scale
        )
        value_part = jnp.einsum(
            "hqk,qhd->khd", probs.astype(LOW_TYPE), grad_block, preferred_element_type=WIDE_TYPE
        )
        grad_query = lax.dynamic_update_slice_in_dim(grad_query, query_part, query_start, 0)
        key_window = lax.dynamic_slice_in_dim(grad_keys, key_start, WINDOW, 0) + key_part
        grad_keys = lax.dynamic_update_slice_in_dim(grad_keys, key_window, key_start, 0)
        value_window = lax.dynamic_slice_in_dim(grad_values, key_start, WINDOW, 0) + value_part
        grad_values = lax.dynamic_update_slice_in_dim(grad_values, value_window, key_start, 0)
        return (grad_query, grad_keys, grad_values)

    zero_field = jnp.zeros(query.shape, WIDE_TYPE)
    return lax.fori_loop(0, row_count // BLOCK, one_block, (zero_field, zero_field, zero_field))


def local(
    patches,
    pos_embed,
    counts,
    ln1_gain,
    w_qkv,
    w_out,
    ln2_gain,
    w_up,
    w_down,
    ln3_gain,
    w_learn1,
    w_learn2,
    cotangent,
):
    row_count = patches.shape[0]
    width = patches.shape[1]
    head_width = w_qkv.shape[2]
    local_heads = head_width // HEAD_DIM
    score_scale = HEAD_DIM ** (-0.5)
    image_count = counts.shape[1]
    token_count = w_learn2.shape[1]
    inputs = patches.astype(WIDE_TYPE) + pos_embed.astype(WIDE_TYPE)
    image_of = image_ids(counts[0], row_count)
    member = (image_of[:, None] == jnp.arange(image_count, dtype=jnp.int32)[None, :]).astype(
        WIDE_TYPE
    )
    row_scale = jnp.sum(member * lax.rsqrt(counts[0].astype(WIDE_TYPE))[None, :], axis=1)
    norm_one, normed_one, inverse_one = layer_norm(inputs, ln1_gain)
    low_one = norm_one.astype(LOW_TYPE)
    qkv = jnp.einsum("td,dch->tch", low_one, w_qkv, preferred_element_type=WIDE_TYPE).astype(
        LOW_TYPE
    )
    query = qkv[:, 0].reshape(row_count, local_heads, HEAD_DIM)
    keys = qkv[:, 1].reshape(row_count, local_heads, HEAD_DIM)
    values = qkv[:, 2].reshape(row_count, local_heads, HEAD_DIM)
    mixed, log_sums = attend_forward(query, keys, values, image_of, score_scale)
    mixed_flat = mixed.reshape(row_count, head_width)
    attended = lax.psum(
        jnp.dot(mixed_flat, w_out, preferred_element_type=WIDE_TYPE).astype(jnp.bfloat16), "tensor"
    ).astype(jnp.float32)
    hidden = inputs + attended
    norm_two, normed_two, inverse_two = layer_norm(hidden, ln2_gain)
    low_two = norm_two.astype(LOW_TYPE)
    upper = jnp.dot(low_two, w_up, preferred_element_type=WIDE_TYPE)
    active = gelu_exact(upper).astype(LOW_TYPE)
    fed = lax.psum(
        jnp.dot(active, w_down, preferred_element_type=WIDE_TYPE).astype(jnp.bfloat16), "tensor"
    ).astype(jnp.float32)
    output = hidden + fed
    norm_three, normed_three, inverse_three = layer_norm(output, ln3_gain)
    low_three = norm_three.astype(LOW_TYPE)
    inner = jnp.dot(low_three, w_learn1, preferred_element_type=WIDE_TYPE)
    acted = gelu_exact(inner).astype(LOW_TYPE)
    logits = jnp.dot(acted, w_learn2, preferred_element_type=WIDE_TYPE)
    select = jax.nn.sigmoid(logits)
    weights = (select * row_scale[:, None]).astype(LOW_TYPE)
    table = (member.astype(LOW_TYPE)[:, :, None] * weights[:, None, :]).reshape(
        row_count, image_count * token_count
    )
    low_out = output.astype(LOW_TYPE)
    pooled = jnp.einsum("tj,td->jd", table, low_out, preferred_element_type=WIDE_TYPE)
    learned = pooled.reshape(image_count, token_count, width).astype(LOW_TYPE)
    grad_pooled = cotangent.reshape(image_count * token_count, width)
    grad_output = jnp.einsum("tj,jd->td", table, grad_pooled, preferred_element_type=WIDE_TYPE)
    grad_table = jnp.einsum("td,jd->tj", low_out, grad_pooled, preferred_element_type=WIDE_TYPE)
    grad_weights = jnp.sum(
        grad_table.reshape(row_count, image_count, token_count) * member[:, :, None], axis=1
    )
    grad_logits = (grad_weights * row_scale[:, None] * select * (1.0 - select)).astype(LOW_TYPE)
    grad_learn2 = jnp.einsum("tl,tk->lk", acted, grad_logits, preferred_element_type=WIDE_TYPE)
    grad_acted = jnp.einsum("tk,lk->tl", grad_logits, w_learn2, preferred_element_type=WIDE_TYPE)
    grad_inner = gelu_grad(inner, grad_acted).astype(LOW_TYPE)
    grad_learn1 = jnp.einsum("td,tl->dl", low_three, grad_inner, preferred_element_type=WIDE_TYPE)
    grad_norm3 = jnp.einsum("tl,dl->td", grad_inner, w_learn1, preferred_element_type=WIDE_TYPE)
    grad_from_three, grad_gain3 = norm_back(grad_norm3, ln3_gain, normed_three, inverse_three)
    grad_output = grad_output + grad_from_three
    grad_fed = grad_output.astype(LOW_TYPE)
    grad_down = jnp.einsum("tf,td->fd", active, grad_fed, preferred_element_type=WIDE_TYPE)
    grad_active = jnp.einsum("td,fd->tf", grad_fed, w_down, preferred_element_type=WIDE_TYPE)
    grad_upper = gelu_grad(upper, grad_active).astype(LOW_TYPE)
    grad_up = jnp.einsum("td,tf->df", low_two, grad_upper, preferred_element_type=WIDE_TYPE)
    grad_norm2 = lax.psum(
        jnp.einsum("tf,df->td", grad_upper, w_up, preferred_element_type=WIDE_TYPE).astype(
            jnp.bfloat16
        ),
        "tensor",
    ).astype(jnp.float32)
    grad_from_two, grad_gain2 = norm_back(grad_norm2, ln2_gain, normed_two, inverse_two)
    grad_hidden = grad_output + grad_from_two
    grad_attended = grad_hidden.astype(LOW_TYPE)
    grad_out_weight = jnp.einsum(
        "th,td->hd", mixed_flat, grad_attended, preferred_element_type=WIDE_TYPE
    )
    grad_mixed = jnp.einsum(
        "td,hd->th", grad_attended, w_out, preferred_element_type=WIDE_TYPE
    ).astype(LOW_TYPE)
    grad_mixed = grad_mixed.reshape(row_count, local_heads, HEAD_DIM)
    grad_query, grad_keys, grad_values = attend_backward(
        query, keys, values, image_of, log_sums, grad_mixed, score_scale
    )
    grad_qkv = (
        jnp.stack([grad_query, grad_keys, grad_values], axis=1)
        .reshape(row_count, 3, head_width)
        .astype(LOW_TYPE)
    )
    grad_qkv_weight = jnp.einsum("td,tch->dch", low_one, grad_qkv, preferred_element_type=WIDE_TYPE)
    grad_norm1 = lax.psum(
        jnp.einsum("tch,dch->td", grad_qkv, w_qkv, preferred_element_type=WIDE_TYPE).astype(
            jnp.bfloat16
        ),
        "tensor",
    ).astype(jnp.float32)
    grad_from_one, grad_gain1 = norm_back(grad_norm1, ln1_gain, normed_one, inverse_one)
    input_grad = (grad_hidden + grad_from_one).astype(LOW_TYPE)
    summed = (
        lax.psum(grad_gain1.astype(jnp.bfloat16), "dp").astype(jnp.float32),
        lax.psum(grad_qkv_weight.astype(jnp.bfloat16), "dp").astype(jnp.float32),
        lax.psum(grad_out_weight.astype(jnp.bfloat16), "dp").astype(jnp.float32),
        lax.psum(grad_gain2.astype(jnp.bfloat16), "dp").astype(jnp.float32),
        lax.psum(grad_up.astype(jnp.bfloat16), "dp").astype(jnp.float32),
        lax.psum(grad_down.astype(jnp.bfloat16), "dp").astype(jnp.float32),
        lax.psum(grad_gain3.astype(jnp.bfloat16), "dp").astype(jnp.float32),
        lax.psum(grad_learn1.astype(jnp.bfloat16), "dp").astype(jnp.float32),
        lax.psum(grad_learn2.astype(jnp.bfloat16), "dp").astype(jnp.float32),
    )
    return (
        learned,
        input_grad,
        summed[0],
        summed[1],
        summed[2],
        summed[3],
        summed[4],
        summed[5],
        summed[6],
        summed[7],
        summed[8],
    )


def solution(mesh):
    return jax.shard_map(
        local,
        mesh=mesh,
        in_specs=(
            P("dp", None),
            P("dp", None),
            P("dp", None),
            P(),
            P(None, None, "tensor"),
            P("tensor", None),
            P(),
            P(None, "tensor"),
            P("tensor", None),
            P(),
            P(),
            P(),
            P("dp", None, None),
        ),
        out_specs=(
            P("dp", None, None),
            P("dp", None),
            P(),
            P(None, None, "tensor"),
            P("tensor", None),
            P(),
            P(None, "tensor"),
            P("tensor", None),
            P(),
            P(),
            P(),
        ),
        check_vma=False,
    )
```

profile of v0, /device:TPU:0, one launch (start us, length us, event | category | flops | bytes accessed | tf_op | source)
XLA Modules:
  0.0 1307.9 jit_solution(3772105733460153413)
XLA Ops:
  21.8 62.9 %while.33 = (s32[]{:T(128)}, bf16[4,512,4,64]{1,3,2,0:T(8,128)(2,1)}, f32[4,4,512,1]{2,1,3,0:T(4,128)}, s32[4]{0:T(128)S(1)}, bf16[2048,4,64]{0,2,1:T(8,128)(2,1...) while((s32[]{:T(128)}, ...), condition=%wide.region_7.8_spmd, body=%wide.region_4.0_spmd.sunk | while | flops 914290688 | bytes 50817812 | solution.py:81
  92.9 157.8 %all-reduce.8.cloned.1.call-done = bf16[2048,1024]{1,0:T(8,128)(2,1)} async-done(((bf16[2048,1024]{1,0:T(8,128)(2,1)}), bf16[2048,1024]{1,0:T(8,128)(2,1)}) %all-reduce.8.cloned.1.call-update) | async-done | bytes 4194320 | tf_op jit(solution)/shard_map/psum | solution.py:159
  261.4 24.0 %multiply_convert_fusion.3 = (bf16[2048,1024]{1,0:T(8,128)(2,1)S(1)}, f32[2048,1024]{1,0:T(8,128)}, f32[2048,1024]{1,0:T(8,128)}) fusion(bf16[2048,1024]{1,0:T(8,128)(2,1)S(1)} %multiply_convert_fusion.4, bf16[1024,1024]{1,0:T(8,128)(2,1)S(1)} %copy-done.55), kind=kOutput, calls=%fused_computation.98 | convolution fusion | flops 4431282176 | bytes 27262976 | tf_op jit(solution)/shard_map/dot_general | solution.py:165
  293.7 153.9 %all-reduce.10.cloned.1.call-done = bf16[2048,1024]{1,0:T(8,128)(2,1)} async-done(((bf16[2048,1024]{1,0:T(8,128)(2,1)}), bf16[2048,1024]{1,0:T(8,128)(2,1)}) %all-reduce.10.cloned.1.call-update) | async-done | bytes 4194320 | tf_op jit(solution)/shard_map/psum | solution.py:167
  455.9 22.9 %multiply_convert_fusion.1 = (bf16[2048,1024]{1,0:T(8,128)(2,1)S(1)}, f32[2048,1024]{1,0:T(8,128)S(1)}, f32[2048,1024]{1,0:T(8,128)}) fusion(bf16[2048,1024]{1,0:T(8,128)(2,1)S(1)} %multiply_convert_fusion.2, bf16[1024,1024]{1,0:T(8,128)(2,1)S(1)} %copy-done), kind=kOutput, calls=%fused_computation.82 | convolution fusion | flops 4431282176 | bytes 27262976 | tf_op jit(solution)/shard_map/dot_general | solution.py:173
  500.0 13.5 %add_convert_fusion = bf16[2048,1024]{1,0:T(8,128)(2,1)S(1)} fusion(f32[2048,1024]{1,0:T(8,128)} %get-tuple-element.421, f32[2048,1024]{1,0:T(8,128)} %get-tuple-element.435, bf16[1024,1024]{1,0:T(8,128)(2,1)S(1)} %copy-done.54, f32[2048,1024]{1,0:T(8,128)} %bitcast_add_fusion), kind=kOutput, calls=%fused_computation.79 | convolution fusion | flops 4326424576 | bytes 31457280 | tf_op jit(solution)/shard_map/td,fd->tf/dot_general | solution.py:200
  523.0 9.7 convolution_convert_fusion.5
  544.8 131.2 %all-reduce.12.cloned.1.call-done = bf16[2048,1024]{1,0:T(8,128)(2,1)} async-done(((bf16[2048,1024]{1,0:T(8,128)(2,1)}), bf16[2048,1024]{1,0:T(8,128)(2,1)}) %all-reduce.12.cloned.1.call-update) | async-done | bytes 4194320 | tf_op jit(solution)/shard_map/psum | solution.py:203
  683.0 7.7 fusion.52
  699.5 255.3 %while.34 = (s32[]{:T(128)}, bf16[2048,4,64]{0,2,1:T(8,128)(2,1)}, f32[2048,4,64]{0,2,1:T(8,128)}, f32[2048,4,64]{0,2,1:T(8,128)}, bf16[2048,4,64]{0,2,1:T(8,128...) while((s32[]{:T(128)}, bf16[2048,4,64]{0,2,1:T(8,128)(2,1)}, ...), condition=%wide.region_23.24_spmd, body=%wide.region_21.23_spmd.sunk | while | flops 2234415104 | bytes 213665648 | solution.py:118
  704.1 9.5 multiply_reduce_fusion.8
  713.6 7.3 multiply_convert_fusion.9
  727.2 10.2 dynamic_update_slice.55
  743.2 10.4 fusion.187
  753.6 10.2 dynamic_update_slice.56
  768.2 9.5 multiply_reduce_fusion.8
  791.3 10.2 dynamic_update_slice.55
  807.3 10.4 fusion.187
  817.7 10.2 dynamic_update_slice.56
  832.3 9.5 multiply_reduce_fusion.8
  855.4 9.8 dynamic_update_slice.55
  871.1 10.4 fusion.187
  881.4 9.8 dynamic_update_slice.56
  895.7 9.5 multiply_reduce_fusion.8
  918.8 9.8 dynamic_update_slice.55
  934.4 10.4 fusion.187
  944.8 9.8 dynamic_update_slice.56
  961.7 9.2 convolution_convert_fusion.7
  986.9 111.4 %all-reduce.16.cloned.1.call-done = (bf16[1024,3,256]{2,0,1:T(8,128)(2,1)}, bf16[256,1024]{1,0:T(8,128)(2,1)}, bf16[1024,1024]{1,0:T(8,128)(2,1)}, bf16[1024,1024]{1,0:T(8,128)(2,1)}, bf16[1024,1024]{1,0:T(8,128)(2,1)}) async-done(((bf16[1024,3,256]{2,0,1:T(8,128)(2,1)}, bf16[256,1024]{1,0:T(8,128)(2,1)}, bf16[1024,1024]{1,0:T(8,128)(2,1)}, bf16[1024,1024]{1,0:T(8,128)(2,1)}, bf16[1024,1024]{1,0:T(8,128)(2,1)}), ...) | async-done | bytes 8388624 | tf_op jit(solution)/shard_map/psum | solution.py:238
  1112.2 144.2 %all-reduce.14.cloned.1.call-done = bf16[2048,1024]{1,0:T(8,128)(2,1)} async-done(((bf16[2048,1024]{1,0:T(8,128)(2,1)}), bf16[2048,1024]{1,0:T(8,128)(2,1)}) %all-reduce.14.cloned.1.call-update) | async-done | bytes 4194320 | tf_op jit(solution)/shard_map/psum | solution.py:228
  1263.4 24.0 %all-reduce = (bf16[1024]{0:T(1024)(128)(2,1)S(1)}, bf16[1024]{0:T(1024)(128)(2,1)S(1)}, bf16[1024]{0:T(1024)(128)(2,1)S(1)}, bf16[1024,8]{0,1:T(8,128)(2,1)S(1)}) all-reduce(bf16[1024]{0:T(1024)(128)(2,1)S(1)} %get-tuple-element.366, bf16[1024]{0:T(1024)(128)(2,1)S(1)} %copy-done.50, ...), channel_id=1, replica_groups=mesh['dp'=8,'tensor'=4] {'dp'}, use_global_device_ids=true, to_apply=%region_28.29 | all-reduce | flops 11264 | bytes 45056 | tf_op jit(solution)/shard_map/psum | solution.py:237
  1289.9 11.2 fusion.58
  (299 shorter events, 301.7 us)
Async XLA Ops:
  7.2 448.7 %copy-start = (bf16[1024,1024]{1,0:T(8,128)(2,1)S(1)}, bf16[1024,1024]{1,0:T(8,128)(2,1)}, u32[]{:S(2)}) copy-start(bf16[1024,1024]{1,0:T(8,128)(2,1)} %param.27) | copy-start | bytes 6291460
  7.2 243.5 %all-reduce.8.cloned.1.call-start = ((), (), s32[]{:S(2)}) async-start(), calls=%async_computation | async-start | bytes 8388608 | tf_op jit(solution)/shard_map/psum | solution.py:159
  84.8 208.9 %copy-start.24 = (s32[2048]{0:T(1024)}, s32[2048]{0:T(1024)S(1)}, u32[]{:S(2)}) copy-start(s32[2048]{0:T(1024)S(1)} %get-tuple-element.686) | copy-start | bytes 24580
  92.9 354.8 %all-reduce.10.cloned.1.call-start = ((), (), s32[]{:S(2)}) async-start(), calls=%async_computation.1 | async-start | bytes 8388608 | tf_op jit(solution)/shard_map/psum | solution.py:167
  258.2 27.1 %copy-start.41 = (f32[2048]{0:T(1024)}, f32[2048]{0:T(1024)S(1)}, u32[]{:S(2)}) copy-start(f32[2048]{0:T(1024)S(1)} %add_rsqrt_fusion.1) | copy-start | bytes 24580
  261.4 24.0 %copy-start.18 = (bf16[2048,1024]{1,0:T(8,128)(2,1)}, bf16[2048,1024]{1,0:T(8,128)(2,1)S(1)}, u32[]{:S(2)}) copy-start(bf16[2048,1024]{1,0:T(8,128)(2,1)S(1)} %multiply_convert_fusion.4) | copy-start | bytes 12582916
  261.4 26.1 %copy-start.53 = (bf16[1024,1024]{1,0:T(8,128)(2,1)S(1)}, bf16[1024,1024]{1,0:T(8,128)(2,1)}, u32[]{:S(2)}) copy-start(bf16[1024,1024]{1,0:T(8,128)(2,1)} %param.25) | copy-start | bytes 6291460
  293.5 382.5 %all-reduce.12.cloned.1.call-start = ((), (), s32[]{:S(2)}) async-start(), calls=%async_computation.2 | async-start | bytes 8388608 | tf_op jit(solution)/shard_map/psum | solution.py:203
  293.7 200.8 %copy-start.37 = (bf16[2048,8]{0,1:T(8,128)(2,1)}, bf16[2048,8]{0,1:T(8,128)(2,1)S(1)}, u32[]{:S(2)}) copy-start(bf16[2048,8]{0,1:T(8,128)(2,1)S(1)} %get-tuple-element.434) | copy-start | bytes 98308
  453.1 41.4 %copy-start.6 = (f32[2048,1024]{1,0:T(8,128)}, f32[2048,1024]{1,0:T(8,128)S(1)}, u32[]{:S(2)}) copy-start(f32[2048,1024]{1,0:T(8,128)S(1)} %get-tuple-element.419) | copy-start | bytes 25165828
  455.9 23.0 %copy-start.20 = (bf16[2048,1024]{1,0:T(8,128)(2,1)}, bf16[2048,1024]{1,0:T(8,128)(2,1)S(1)}, u32[]{:S(2)}) copy-start(bf16[2048,1024]{1,0:T(8,128)(2,1)S(1)} %multiply_convert_fusion.2) | copy-start | bytes 12582916
  455.9 22.9 %copy-start.58 = (bf16[8,8,1024]{2,1,0:T(8,128)(2,1)S(1)}, bf16[8,8,1024]{2,1,0:T(8,128)(2,1)}, u32[]{:S(2)}) copy-start(bf16[8,8,1024]{2,1,0:T(8,128)(2,1)} %param.29) | copy-start | bytes 393220
  481.5 13.0 copy-start.33
  500.0 15.6 %copy-start.56 = (bf16[1024,1024]{1,0:T(8,128)(2,1)S(1)}, bf16[1024,1024]{1,0:T(8,128)(2,1)}, u32[]{:S(2)}) copy-start(bf16[1024,1024]{1,0:T(8,128)(2,1)} %param.24) | copy-start | bytes 6291460
  521.9 576.4 %all-reduce.16.cloned.1.call-start = ((), (), s32[]{:S(2)}) async-start(), calls=%async_computation.4 | async-start | bytes 16777216 | tf_op jit(solution)/shard_map/psum | solution.py:238
  523.0 15.9 %slice-start = ((s8[8388608]{0:T(1024)(128)(4,1)}), s8[4194304]{0:T(1024)(128)(4,1)S(1)}, s32[]{:S(2)}) async-start(s8[8388608]{0:T(1024)(128)(4,1)} %bitcast.122), calls=%async_computation.5 | async-start | bytes 8388608
  539.0 137.1 %copy-start.32 = (f32[2048]{0:T(1024)S(1)}, f32[2048]{0:T(1024)}, u32[]{:S(2)}) copy-start(f32[2048]{0:T(1024)} %copy-done.31) | copy-start | bytes 24580
  539.0 137.1 %copy-start.42 = (f32[2048]{0:T(1024)S(1)}, f32[2048]{0:T(1024)}, u32[]{:S(2)}) copy-start(f32[2048]{0:T(1024)} %copy-done.41) | copy-start | bytes 24580
  539.0 137.0 %copy-start.46 = (f32[1024]{0:T(1024)S(1)}, f32[1024]{0:T(1024)}, u32[]{:S(2)}) copy-start(f32[1024]{0:T(1024)} %param.23) | copy-start | bytes 12292
  702.7 10.9 copy-start.2
  713.6 10.1 copy-start.11
  766.8 10.9 copy-start.2
  777.7 10.1 copy-start.11
  830.9 10.9 copy-start.2
  841.8 10.1 copy-start.11
  894.2 11.0 copy-start.2
  905.2 10.1 copy-start.11
  971.0 285.4 %all-reduce.14.cloned.1.call-start = ((), (), s32[]{:S(2)}) async-start(), calls=%async_computation.3 | async-start | bytes 8388608 | tf_op jit(solution)/shard_map/psum | solution.py:228
  1098.3 10.8 copy-start.26
  1109.2 154.2 %copy-start.50 = (bf16[1024]{0:T(1024)(128)(2,1)S(1)}, bf16[1024]{0:T(1024)(128)(2,1)}, u32[]{:S(2)}) copy-start(bf16[1024]{0:T(1024)(128)(2,1)} %get-tuple-element.364) | copy-start | bytes 6148
  1109.2 154.2 %copy-start.52 = (bf16[1024]{0:T(1024)(128)(2,1)S(1)}, bf16[1024]{0:T(1024)(128)(2,1)}, u32[]{:S(2)}) copy-start(bf16[1024]{0:T(1024)(128)(2,1)} %get-tuple-element.362) | copy-start | bytes 6148
  1289.8 11.2 copy-start.1
  (53 other events, 256.9 us)
Sparse Core Ops, SparseCore 0:
  93.0 157.6 all-reduce.7
  293.6 153.9 all-reduce.9
  522.0 153.9 all-reduce.11
  971.1 127.1 all-reduce.15
  1101.1 155.2 all-reduce.13
where the time goes:
time: 1320 us; the launch traced here: 1310 us
  waiting for transfers between devices  699 us (53%)
  matrix products  319 us (24%)
  other arithmetic  128 us (10%)
  local copies, waits for them, and re-layouts  119 us (9%)
  blocking collectives  24 us (2%)
  between operations  14.9 us (1%)
    psum x1, waiting for transfers between devices, local(): lax.psum(jnp.dot(mixed_flat, w_out, preferred_element_type=WIDE_TYPE).ast...  158 us
    psum x1, waiting for transfers between devices, local(): lax.psum(jnp.dot(active, w_down, preferred_element_type=WIDE_TYPE).astype...  154 us
    psum x1, waiting for transfers between devices, local(): lax.psum(jnp.einsum('tch,dch->td', grad_qkv, w_qkv, preferred_element_typ...  144 us
    psum x1, waiting for transfers between devices, local(): lax.psum(jnp.einsum('tf,df->td', grad_upper, w_up, preferred_element_type...  131 us
    psum x1, waiting for transfers between devices, local(): lax.psum(grad_qkv_weight.astype(jnp.bfloat16), 'dp').astype(jnp.float32)  111 us
    dot_general x4, matrix products, one_block(): jnp.einsum('hqk,qhd->khd', probs.astype(LOW_TYPE), grad_block, preferred_...  41.5 us
    dynamic_update_slice x4, local copies, waits for them, and re-layouts, one_block(): lax.dynamic_update_slice_in_dim(grad_values, value_window, key_start, 0)  40 us
    dynamic_update_slice x4, local copies, waits for them, and re-layouts, one_block(): lax.dynamic_update_slice_in_dim(grad_keys, key_window, key_start, 0)  40 us
  transfers between devices with their start and end apart: 5, of which 5 were waited for; matrix products, arithmetic and copies ran while one was open for 4% of the time, Pallas kernels for 0%

commit v1 on v0

--- a/solution.py
+++ b/solution.py
@@ -2,6 +2,7 @@
 import jax.numpy as jnp
 from jax import lax
 from jax.sharding import PartitionSpec as P
+from jax.lax import all_gather
 
 HEAD_DIM = 64
 MOST = 576
@@ -235,7 +236,7 @@
     input_grad = (grad_hidden + grad_from_one).astype(LOW_TYPE)
     summed = (
         lax.psum(grad_gain1.astype(jnp.bfloat16), "dp").astype(jnp.float32),
-        lax.psum(grad_qkv_weight.astype(jnp.bfloat16), "dp").astype(jnp.float32),
+        jnp.sum(all_gather(grad_qkv_weight.astype(jnp.bfloat16), "dp"), axis=0).astype(jnp.float32),
         lax.psum(grad_out_weight.astype(jnp.bfloat16), "dp").astype(jnp.float32),
         lax.psum(grad_gain2.astype(jnp.bfloat16), "dp").astype(jnp.float32),
         lax.psum(grad_up.astype(jnp.bfloat16), "dp").astype(jnp.float32),

time: 1320 us -> 1240 us (0.939)
  waiting for transfers between devices: 699 us -> 596 us
    psum x1, waiting for transfers between devices: 111 us -> 0.01 us  [local(): lax.psum(grad_out_weight.astype(jnp.bfloat16), 'dp').astype(jnp.float32)]
    all_gather x0 -> x1, waiting for transfers between devices: none -> 27.2 us  [local(): all_gather(grad_qkv_weight.astype(jnp.bfloat16), 'dp')]
    psum x1, waiting for transfers between devices: 144 us -> 126 us  [local(): lax.psum(jnp.einsum('tch,dch->td', grad_qkv, w_qkv, preferred_element_typ...]
  transfers between devices with their start and end apart: 5 -> 6, of which waited for: 5 -> 5; matrix products, arithmetic and copies ran while one was open for 4% -> 27% of each run, Pallas kernels for 0% -> 0%
where the time goes in v1:
time: 1240 us; the launch traced here: 1220 us
  waiting for transfers between devices  596 us (48%)
  matrix products  324 us (26%)
  other arithmetic  139 us (11%)
  local copies, waits for them, and re-layouts  120 us (10%)
  blocking collectives  24.7 us (2%)
  between operations  15.3 us (1%)
    psum x1, waiting for transfers between devices, local(): lax.psum(jnp.dot(mixed_flat, w_out, preferred_element_type=WIDE_TYPE).ast...  158 us
    psum x1, waiting for transfers between devices, local(): lax.psum(jnp.dot(active, w_down, preferred_element_type=WIDE_TYPE).astype...  154 us
    psum x1, waiting for transfers between devices, local(): lax.psum(jnp.einsum('tf,df->td', grad_upper, w_up, preferred_element_type...  131 us
    psum x1, waiting for transfers between devices, local(): lax.psum(jnp.einsum('tch,dch->td', grad_qkv, w_qkv, preferred_element_typ...  126 us
    dot_general x4, matrix products, one_block(): jnp.einsum('hqk,qhd->khd', probs.astype(LOW_TYPE), grad_block, preferred_...  41.7 us
    dynamic_update_slice x4, local copies, waits for them, and re-layouts, one_block(): lax.dynamic_update_slice_in_dim(grad_values, value_window, key_start, 0)  40.2 us
    dynamic_update_slice x4, local copies, waits for them, and re-layouts, one_block(): lax.dynamic_update_slice_in_dim(grad_keys, key_window, key_start, 0)  40.1 us
    dot_general x4, matrix products, one_block(): jnp.einsum('qhd,khd->hqk', grad_block, value_block, preferred_element_typ...  38.3 us
  transfers between devices with their start and end apart: 6, of which 5 were waited for; matrix products, arithmetic and copies ran while one was open for 27% of the time, Pallas kernels for 0%

profile of v1, /device:TPU:0, one launch (start us, length us, event | category | flops | bytes accessed | tf_op | source)
XLA Modules:
  0.0 1223.3 jit_solution(713076502923570012)
XLA Ops:
  21.8 62.9 %while.33 = (s32[]{:T(128)}, bf16[4,512,4,64]{1,3,2,0:T(8,128)(2,1)}, f32[4,4,512,1]{2,1,3,0:T(4,128)}, s32[4]{0:T(128)S(1)}, bf16[2048,4,64]{0,2,1:T(8,128)(2,1...) while((s32[]{:T(128)}, ...), condition=%wide.region_7.8_spmd, body=%wide.region_4.0_spmd.sunk | while | flops 914290688 | bytes 50817812 | solution.py:82
  92.9 157.8 %all-reduce.8.cloned.1.call-done = bf16[2048,1024]{1,0:T(8,128)(2,1)} async-done(((bf16[2048,1024]{1,0:T(8,128)(2,1)}), bf16[2048,1024]{1,0:T(8,128)(2,1)}) %all-reduce.8.cloned.1.call-update) | async-done | bytes 4194320 | tf_op jit(solution)/shard_map/psum | solution.py:160
  261.4 24.0 %multiply_convert_fusion.3 = (bf16[2048,1024]{1,0:T(8,128)(2,1)S(1)}, f32[2048,1024]{1,0:T(8,128)}, f32[2048,1024]{1,0:T(8,128)}) fusion(bf16[2048,1024]{1,0:T(8,128)(2,1)S(1)} %multiply_convert_fusion.4, bf16[1024,1024]{1,0:T(8,128)(2,1)S(1)} %copy-done.53), kind=kOutput, calls=%fused_computation.98 | convolution fusion | flops 4431282176 | bytes 27262976 | tf_op jit(solution)/shard_map/dot_general | solution.py:166
  293.7 153.9 %all-reduce.10.cloned.1.call-done = bf16[2048,1024]{1,0:T(8,128)(2,1)} async-done(((bf16[2048,1024]{1,0:T(8,128)(2,1)}), bf16[2048,1024]{1,0:T(8,128)(2,1)}) %all-reduce.10.cloned.1.call-update) | async-done | bytes 4194320 | tf_op jit(solution)/shard_map/psum | solution.py:168
  455.9 22.9 %multiply_convert_fusion.1 = (bf16[2048,1024]{1,0:T(8,128)(2,1)S(1)}, f32[2048,1024]{1,0:T(8,128)S(1)}, f32[2048,1024]{1,0:T(8,128)}) fusion(bf16[2048,1024]{1,0:T(8,128)(2,1)S(1)} %multiply_convert_fusion.2, bf16[1024,1024]{1,0:T(8,128)(2,1)S(1)} %copy-done), kind=kOutput, calls=%fused_computation.82 | convolution fusion | flops 4431282176 | bytes 27262976 | tf_op jit(solution)/shard_map/dot_general | solution.py:174
  499.9 13.6 %add_convert_fusion = bf16[2048,1024]{1,0:T(8,128)(2,1)S(1)} fusion(f32[2048,1024]{1,0:T(8,128)} %get-tuple-element.420, f32[2048,1024]{1,0:T(8,128)} %get-tuple-element.434, bf16[1024,1024]{1,0:T(8,128)(2,1)S(1)} %copy-done.52, f32[2048,1024]{1,0:T(8,128)} %bitcast_add_fusion), kind=kOutput, calls=%fused_computation.79 | convolution fusion | flops 4326424576 | bytes 31457280 | tf_op jit(solution)/shard_map/td,fd->tf/dot_general | solution.py:201
  523.0 9.7 convolution_convert_fusion.5
  544.8 131.3 %all-reduce.12.cloned.1.call-done = bf16[2048,1024]{1,0:T(8,128)(2,1)} async-done(((bf16[2048,1024]{1,0:T(8,128)(2,1)}), bf16[2048,1024]{1,0:T(8,128)(2,1)}) %all-reduce.12.cloned.1.call-update) | async-done | bytes 4194320 | tf_op jit(solution)/shard_map/psum | solution.py:204
  683.0 7.7 fusion.52
  705.0 256.6 %while.34 = (s32[]{:T(128)}, bf16[2048,4,64]{0,2,1:T(8,128)(2,1)}, f32[2048,4,64]{0,2,1:T(8,128)}, f32[2048,4,64]{0,2,1:T(8,128)}, bf16[2048,4,64]{0,2,1:T(8,128...) while((s32[]{:T(128)}, bf16[2048,4,64]{0,2,1:T(8,128)(2,1)}, ...), condition=%wide.region_23.24_spmd, body=%wide.region_21.23_spmd.sunk | while | flops 2234415104 | bytes 213665648 | solution.py:119
  709.6 9.5 multiply_reduce_fusion.8
  732.9 10.3 dynamic_update_slice.55
  749.0 10.6 fusion.187
  759.6 10.4 dynamic_update_slice.56
  774.4 9.9 multiply_reduce_fusion.8
  798.0 10.3 dynamic_update_slice.55
  814.1 10.4 fusion.187
  824.5 10.2 dynamic_update_slice.56
  839.2 9.5 multiply_reduce_fusion.8
  862.2 9.8 dynamic_update_slice.55
  877.9 10.4 fusion.187
  888.3 9.8 dynamic_update_slice.56
  902.5 9.5 multiply_reduce_fusion.8
  925.6 9.8 dynamic_update_slice.55
  941.2 10.4 fusion.187
  951.6 9.8 dynamic_update_slice.56
  976.2 9.1 convolution_convert_fusion.7
  1004.9 125.9 %all-reduce.14.cloned.1.call-done = bf16[2048,1024]{1,0:T(8,128)(2,1)} async-done(((bf16[2048,1024]{1,0:T(8,128)(2,1)}), bf16[2048,1024]{1,0:T(8,128)(2,1)}) %all-reduce.14.cloned.1.call-update) | async-done | bytes 4194320 | tf_op jit(solution)/shard_map/psum | solution.py:229
  1138.0 24.7 %all-reduce = (bf16[1024]{0:T(1024)(128)(2,1)S(1)}, bf16[1024]{0:T(1024)(128)(2,1)S(1)}, bf16[1024]{0:T(1024)(128)(2,1)S(1)}, bf16[1024,8]{0,1:T(8,128)(2,1)S(1)}) all-reduce(bf16[1024]{0:T(1024)(128)(2,1)S(1)} %get-tuple-element.366, bf16[1024]{0:T(1024)(128)(2,1)S(1)} %copy-done.48, ...), channel_id=1, replica_groups=mesh['dp'=8,'tensor'=4] {'dp'}, use_global_device_ids=true, to_apply=%region_28.29 | all-reduce | flops 11264 | bytes 45056 | tf_op jit(solution)/shard_map/psum | solution.py:238
  1165.1 12.3 %fusion.58 = bf16[2048,1024]{1,0:T(8,128)(2,1)} fusion(f32[2048,1024]{1,0:T(8,128)} %copy-done.5, bf16[2048,1024]{1,0:T(8,128)(2,1)} %all-reduce.14.cloned.1.call-done, f32[2048]{0:T(1024)S(1)} %broadcast_multiply_fusion, f32[2048]{0:T(1024)S(1)} %broadcast_multiply_fusion.1, f32[1024]{0:T(1024)S(1)} %copy-done.47, f32[2048]{0:T(1024)S(1)} %copy-done.42, ...), kind=kLoop, calls=%fused_computation.71 | loop fusion | flops 27262976 | bytes 25202688 | tf_op jit(solution)/shard_map/convert_element_type | solution.py:236
  1177.4 27.2 %all-gather.3.cloned.1.call-done = bf16[8192,3,256]{2,0,1:T(8,128)(2,1)} async-done(((bf16[1024,3,256]{2,0,1:T(8,128)(2,1)}), bf16[8192,3,256]{2,0,1:T(8,128)(2,1)}) %all-gather.3.cloned.1.call-update) | async-done | bytes 12582928 | tf_op jit(solution)/shard_map/all_gather | solution.py:239
  1204.6 8.0 reduce_sum.218
  (299 shorter events, 316.2 us)
Async XLA Ops:
  7.2 448.7 %copy-start = (bf16[1024,1024]{1,0:T(8,128)(2,1)S(1)}, bf16[1024,1024]{1,0:T(8,128)(2,1)}, u32[]{:S(2)}) copy-start(bf16[1024,1024]{1,0:T(8,128)(2,1)} %param.27) | copy-start | bytes 6291460
  7.2 243.5 %all-reduce.8.cloned.1.call-start = ((), (), s32[]{:S(2)}) async-start(), calls=%async_computation | async-start | bytes 8388608 | tf_op jit(solution)/shard_map/psum | solution.py:160
  84.8 208.9 %copy-start.24 = (s32[2048]{0:T(1024)}, s32[2048]{0:T(1024)S(1)}, u32[]{:S(2)}) copy-start(s32[2048]{0:T(1024)S(1)} %get-tuple-element.685) | copy-start | bytes 24580
  92.9 354.8 %all-reduce.10.cloned.1.call-start = ((), (), s32[]{:S(2)}) async-start(), calls=%async_computation.1 | async-start | bytes 8388608 | tf_op jit(solution)/shard_map/psum | solution.py:168
  258.3 27.1 %copy-start.39 = (f32[2048]{0:T(1024)}, f32[2048]{0:T(1024)S(1)}, u32[]{:S(2)}) copy-start(f32[2048]{0:T(1024)S(1)} %add_rsqrt_fusion.1) | copy-start | bytes 24580
  261.4 24.0 %copy-start.18 = (bf16[2048,1024]{1,0:T(8,128)(2,1)}, bf16[2048,1024]{1,0:T(8,128)(2,1)S(1)}, u32[]{:S(2)}) copy-start(bf16[2048,1024]{1,0:T(8,128)(2,1)S(1)} %multiply_convert_fusion.4) | copy-start | bytes 12582916
  261.4 26.1 %copy-start.51 = (bf16[1024,1024]{1,0:T(8,128)(2,1)S(1)}, bf16[1024,1024]{1,0:T(8,128)(2,1)}, u32[]{:S(2)}) copy-start(bf16[1024,1024]{1,0:T(8,128)(2,1)} %param.25) | copy-start | bytes 6291460
  293.5 382.5 %all-reduce.12.cloned.1.call-start = ((), (), s32[]{:S(2)}) async-start(), calls=%async_computation.2 | async-start | bytes 8388608 | tf_op jit(solution)/shard_map/psum | solution.py:204
  293.7 200.8 %copy-start.35 = (bf16[2048,8]{0,1:T(8,128)(2,1)}, bf16[2048,8]{0,1:T(8,128)(2,1)S(1)}, u32[]{:S(2)}) copy-start(bf16[2048,8]{0,1:T(8,128)(2,1)S(1)} %get-tuple-element.433) | copy-start | bytes 98308
  453.1 41.4 %copy-start.6 = (f32[2048,1024]{1,0:T(8,128)}, f32[2048,1024]{1,0:T(8,128)S(1)}, u32[]{:S(2)}) copy-start(f32[2048,1024]{1,0:T(8,128)S(1)} %get-tuple-element.418) | copy-start | bytes 25165828
  455.9 23.0 %copy-start.20 = (bf16[2048,1024]{1,0:T(8,128)(2,1)}, bf16[2048,1024]{1,0:T(8,128)(2,1)S(1)}, u32[]{:S(2)}) copy-start(bf16[2048,1024]{1,0:T(8,128)(2,1)S(1)} %multiply_convert_fusion.2) | copy-start | bytes 12582916
  455.9 23.0 %copy-start.56 = (bf16[8,8,1024]{2,1,0:T(8,128)(2,1)S(1)}, bf16[8,8,1024]{2,1,0:T(8,128)(2,1)}, u32[]{:S(2)}) copy-start(bf16[8,8,1024]{2,1,0:T(8,128)(2,1)} %param.29) | copy-start | bytes 393220
  481.5 13.0 %copy-start.31 = (bf16[2048,8]{0,1:T(8,128)(2,1)}, bf16[2048,8]{0,1:T(8,128)(2,1)S(1)}, u32[]{:S(2)}) copy-start(bf16[2048,8]{0,1:T(8,128)(2,1)S(1)} %get-tuple-element.431) | copy-start | bytes 98308
  499.9 15.6 %copy-start.54 = (bf16[1024,1024]{1,0:T(8,128)(2,1)S(1)}, bf16[1024,1024]{1,0:T(8,128)(2,1)}, u32[]{:S(2)}) copy-start(bf16[1024,1024]{1,0:T(8,128)(2,1)} %param.24) | copy-start | bytes 6291460
  521.9 471.1 %all-reduce.16.cloned.1.call-start = ((), (), s32[]{:S(2)}) async-start(), calls=%async_computation.5 | async-start | bytes 13631488 | tf_op jit(solution)/shard_map/psum | solution.py:240
  523.0 15.9 %slice-start = ((s8[8388608]{0:T(1024)(128)(4,1)}), s8[4194304]{0:T(1024)(128)(4,1)S(1)}, s32[]{:S(2)}) async-start(s8[8388608]{0:T(1024)(128)(4,1)} %bitcast.124), calls=%async_computation.6 | async-start | bytes 8388608
  538.9 137.1 %copy-start.30 = (f32[2048]{0:T(1024)S(1)}, f32[2048]{0:T(1024)}, u32[]{:S(2)}) copy-start(f32[2048]{0:T(1024)} %copy-done.29) | copy-start | bytes 24580
  538.9 137.1 %copy-start.40 = (f32[2048]{0:T(1024)S(1)}, f32[2048]{0:T(1024)}, u32[]{:S(2)}) copy-start(f32[2048]{0:T(1024)} %copy-done.39) | copy-start | bytes 24580
  539.0 137.1 %copy-start.44 = (f32[1024]{0:T(1024)S(1)}, f32[1024]{0:T(1024)}, u32[]{:S(2)}) copy-start(f32[1024]{0:T(1024)} %param.23) | copy-start | bytes 12292
  683.0 11.1 copy-start.17
  701.8 428.9 %all-reduce.14.cloned.1.call-start = ((), (), s32[]{:S(2)}) async-start(), calls=%async_computation.3 | async-start | bytes 8388608 | tf_op jit(solution)/shard_map/psum | solution.py:229
  708.2 10.9 copy-start.2
  772.9 11.3 copy-start.2
  837.7 10.9 copy-start.2
  901.0 10.9 copy-start.2
  976.0 12.1 copy-start.32
  976.1 12.0 copy-start.36
  976.1 228.5 %all-gather.3.cloned.1.call-start = ((), (), s32[]{:S(2)}) async-start(), calls=%async_computation.4 | async-start | bytes 14155776 | tf_op jit(solution)/shard_map/all_gather | solution.py:239
  993.0 10.8 copy-start.28
  1003.8 134.2 %copy-start.48 = (bf16[1024]{0:T(1024)(128)(2,1)S(1)}, bf16[1024]{0:T(1024)(128)(2,1)}, u32[]{:S(2)}) copy-start(bf16[1024]{0:T(1024)(128)(2,1)} %get-tuple-element.364) | copy-start | bytes 6148
  1003.8 134.2 %copy-start.50 = (bf16[1024]{0:T(1024)(128)(2,1)S(1)}, bf16[1024]{0:T(1024)(128)(2,1)}, u32[]{:S(2)}) copy-start(bf16[1024]{0:T(1024)(128)(2,1)} %get-tuple-element.362) | copy-start | bytes 6148
  1204.6 11.4 copy-start.1
  (52 other events, 283.6 us)
Sparse Core Ops, SparseCore 0:
  93.0 157.6 all-reduce.7
  293.6 153.9 all-reduce.9
  522.0 153.9 all-reduce.11
  701.9 109.6 all-reduce.15
  976.2 154.5 all-reduce.13
  1133.2 71.3 all-gather.2
